TPU v7x, 32 devices: a whole 2x2x4 slice. The times are simulated.
32 devices in a mesh: ax: 8 (over y, x, core), circ: 4 (over z).
Axes of the slice: x: 2, y: 2, z: 4, core: 2. Of those that a mesh axis runs over, the one named last changes fastest.
Arguments:
- endothelium: float32 [3, 32, 512, 128], P(None, 'ax', 'circ'), may hold values from -6 to 6
- muscle: float32 [3, 64, 256, 128], P(None, 'ax', 'circ'), may hold values from -6 to 6
- agonist: float32 [32, 512, 128], P('ax', 'circ'), may hold values from 0.2 to 2
- proj_cell: int32 [32, 32, 2], P(('ax', 'circ')), may hold values from 0 to 511
- proj_target: int32 [32, 32, 2], P(('ax', 'circ')), may hold values from 0 to 511
- proj_count: int32 [32, 32], P(('ax', 'circ')), may hold values from 0 to 2, as said below
- endo_inverse: float32 [3, 128, 128], replicated, may hold values from 0 to 0.29
- muscle_inverse: float32 [3, 128, 128], replicated, may hold values from 0 to 0.43
Outputs:
- endo_next: float32 [3, 32, 512, 128], P(None, 'ax', 'circ')
- muscle_next: float32 [3, 64, 256, 128], P(None, 'ax', 'circ')
Inputs may be any that keep to these rules, and one draw needn't show every extreme that they name: `proj_count`: the live slots of a pair are its first ones. In every draw some owner receives 2 from every device and some device sends 2 to every owner.
All inputs are finite; a program needn't handle non-finite values.
Results may differ from a plain program's by a relative error of at most 0.0001.
Values sent between devices are 32-bit elements; how exact they have to be, the bound alone decides.
A program may use at most 64 MiB of HBM per device.

v0:
```python
import functools

import jax
import jax.numpy as jnp
from jax import lax
from jax.experimental import pallas as pl
from jax.experimental.pallas import tpu as pltpu
from jax.sharding import PartitionSpec as P

MESH = pl.DeviceIdType.MESH
TIME_STEPS = 8
DT = 0.2
COUPLING = (0.1, 0.3, 0.5)
ENDO_GAP = (0.05, 0.3, 0.5)
MUSC_GAP = (0.05, 0.1, 0.4)
BF16 = jnp.bfloat16
F32 = jnp.float32


def halves(x):
    high = x.astype(BF16)
    return high, (x - high.astype(F32)).astype(BF16)


def side_by_side(x):
    return jnp.concatenate(halves(x), axis=1)


def folded(y):
    half = y.shape[1] // 2
    return y[:, :half] + y[:, half:]


def dot(a, b):
    return jnp.dot(a, b, preferred_element_type=F32)


def reaction(u0, u1, u2, drive):
    square = u1 * u1
    release = square / (0.5 + square)
    second = -0.5 * u1 if drive is None else drive - 0.5 * u1
    return (1.2 * release - 0.6 * u0 - 0.2 * u2, second, 0.5 * u0 - 0.8 * u2)


def kernel(
    sizes,
    endo_in, musc_in, agonist, endo_col, endo_row, musc_col, musc_row, endo_inv, musc_inv,
    endo_out, musc_out,
    endo, musc, halo_low, halo_high, edge_out, edge_left, edge_right,
    send, recv, picked, weights, take_e, take_m, put_e, put_m, rhs,
    in_sems, own_sem, send_sem, recv_sem, halo_send, halo_recv, edge_send, edge_recv,
):
    n_ax, n_circ, width, length, cycle = sizes
    n = n_ax * n_circ
    points = endo.shape[3]
    rows = endo.shape[2]
    musc_rows = musc.shape[2]
    ax = lax.axis_index("ax")
    circ = lax.axis_index("circ")
    me = ax * n_circ + circ
    right = lax.rem(circ + 1, n_circ)
    left = lax.rem(circ + n_circ - 1, n_circ)

    def place(p):
        return (p // n_circ, lax.rem(p, n_circ))

    load_e = pltpu.make_async_copy(endo_in, endo.at[0], in_sems.at[0])
    load_m = pltpu.make_async_copy(musc_in, musc.at[0], in_sems.at[1])
    load_e.start()
    load_m.start()

    barrier = pltpu.get_barrier_semaphore()

    def greet(k, carry):
        p = lax.rem(me + k, n)
        pl.semaphore_signal(barrier, inc=1, device_id=place(p), device_id_type=MESH)
        return carry

    lax.fori_loop(1, n, greet, 0)

    for layer, inv in ((0, endo_inv), (1, musc_inv)):
        for s in range(3):
            row = side_by_side(inv[s].T)
            weights[layer * 3 + s] = jnp.concatenate([row, row], axis=0)
    for col, row, take, put, count in (
        (endo_col, endo_row, take_e, put_e, rows), (musc_col, musc_row, take_m, put_m, musc_rows),
    ):
        ids = lax.broadcasted_iota(jnp.int32, take.shape, 1)
        take[...] = jnp.where(ids == col[...], 1.0, 0.0).astype(BF16)
        ids = lax.broadcasted_iota(jnp.int32, put.shape, 0)
        put[...] = jnp.where(ids == row[...], 1.0, 0.0).astype(BF16)

    @pl.when(ax == 0)
    def _():
        halo_low[...] = jnp.zeros_like(halo_low)

    @pl.when(ax == n_ax - 1)
    def _():
        halo_high[...] = jnp.zeros_like(halo_high)

    load_e.wait()
    load_m.wait()
    pl.semaphore_wait(barrier, n - 1)

    def step(t, carry):
        par = lax.rem(t, 2)
        nxt = 1 - par

        def to(p):
            return pltpu.make_async_remote_copy(
                src_ref=send.at[p, pl.ds(0, 12)],
                dst_ref=recv.at[par, me, pl.ds(0, 12)],
                send_sem=send_sem,
                recv_sem=recv_sem.at[par],
                device_id=place(p),
                device_id_type=MESH,
            )

        low = pltpu.make_async_remote_copy(
            src_ref=endo.at[par, :, pl.ds(0, width)], dst_ref=halo_high.at[par],
            send_sem=halo_send.at[0], recv_sem=halo_recv.at[par, 0],
            device_id=(ax - 1, circ), device_id_type=MESH,
        )
        high = pltpu.make_async_remote_copy(
            src_ref=endo.at[par, :, pl.ds(rows - width, width)], dst_ref=halo_low.at[par],
            send_sem=halo_send.at[1], recv_sem=halo_recv.at[par, 1],
            device_id=(ax + 1, circ), device_id_type=MESH,
        )
        to_left = pltpu.make_async_remote_copy(
            src_ref=edge_out.at[0], dst_ref=edge_right.at[par],
            send_sem=edge_send.at[0], recv_sem=edge_recv.at[par, 0],
            device_id=(ax, left), device_id_type=MESH,
        )
        to_right = pltpu.make_async_remote_copy(
            src_ref=edge_out.at[1], dst_ref=edge_left.at[par],
            send_sem=edge_send.at[1], recv_sem=edge_recv.at[par, 1],
            device_id=(ax, right), device_id_type=MESH,
        )

        flat = send.reshape(n * 16, points)
        for layer, state, take in ((0, endo, take_e), (1, musc, take_m)):
            for s in range(3):
                got = folded(dot(take[...], side_by_side(state[par, s])))
                picked[layer * 3 + s] = got
                for slot in range(2):
                    k = layer * 6 + s * 2 + slot
                    flat[pl.ds(k, n, stride=16), :] = got[slot * n:(slot + 1) * n]
        for s in range(3):
            edge_out[0, pl.ds(s * length, length)] = musc[par, s, pl.ds(0, length, stride=cycle), :]
            edge_out[1, pl.ds(s * length, length)] = musc[
                par, s, pl.ds(cycle - 1, length, stride=cycle), :
            ]

        @pl.when(ax > 0)
        def _():
            low.start()

        @pl.when(ax < n_ax - 1)
        def _():
            high.start()

        def launch(k, carry):
            to(lax.rem(me + k, n)).start()
            return carry

        lax.fori_loop(1, n, launch, 0)
        to_left.start()
        to_right.start()
        own = pltpu.make_async_copy(
            send.at[me, pl.ds(0, 12)], recv.at[par, me, pl.ds(0, 12)], own_sem
        )
        own.start()

        count = rows // width
        for a in range(count):
            for j in range(0, width, 64):
                here = pl.ds(a * width + j, 64)
                u = [endo[par, s, here, :] for s in range(3)]
                parts = reaction(u[0], u[1], u[2], agonist[here, :])
                for s in range(3):
                    lap = -2.0 * u[s]
                    if a > 0:
                        lap = lap + endo[par, s, pl.ds((a - 1) * width + j, 64), :]
                    if a < count - 1:
                        lap = lap + endo[par, s, pl.ds((a + 1) * width + j, 64), :]
                    value = u[s] + DT * (parts[s] + ENDO_GAP[s] * lap)
                    rhs[s, here, :] = side_by_side(value)

        def musc_base(a, carry):
            here = pl.ds(pl.multiple_of(a * cycle, cycle), cycle)
            place_in = lax.broadcasted_iota(jnp.int32, (cycle, points), 0)
            u = [musc[par, s, here, :] for s in range(3)]
            parts = reaction(u[0], u[1], u[2], None)
            for s in range(3):
                before = jnp.where(place_in == 0, 0.0, pltpu.roll(u[s], 1, 0))
                after = jnp.where(place_in == cycle - 1, 0.0, pltpu.roll(u[s], cycle - 1, 0))
                lap = before + after - 2.0 * u[s]
                value = u[s] + DT * (parts[s] + MUSC_GAP[s] * lap)
                rhs[3 + s, here, :] = side_by_side(value)
            return carry

        lax.fori_loop(0, length, musc_base, 0)

        for s in range(3):
            endo[nxt, s] = folded(dot(rhs[s], weights[s]))
            musc[nxt, s] = folded(dot(rhs[3 + s], weights[3 + s]))

        own.wait()
        every = pltpu.make_async_remote_copy(
            src_ref=send.at[pl.ds(0, n - 1), pl.ds(0, 12)],
            dst_ref=recv.at[par, pl.ds(0, n - 1), pl.ds(0, 12)],
            send_sem=send_sem, recv_sem=recv_sem.at[par],
            device_id=(ax, right), device_id_type=MESH,
        )
        every.wait_recv()
        to_left.wait_recv()
        to_right.wait_recv()

        @pl.when(ax > 0)
        def _():
            high.wait_recv()

        @pl.when(ax < n_ax - 1)
        def _():
            low.wait_recv()

        def arrived(layer, s):
            flat_in = recv.at[par].reshape(n * 16, points)
            k = layer * 6 + s * 2
            return jnp.concatenate(
                [flat_in[pl.ds(k + slot, n, stride=16), :] for slot in range(2)], axis=0
            )

        endo_flux, musc_flux, lows, highs, lefts, rights = [], [], [], [], [], []
        for s in range(3):
            flux = (DT * COUPLING[s]) * (arrived(1, s) - picked[s])
            gap = DT * ENDO_GAP[s]
            block = jnp.concatenate([gap * halo_low[par, s], gap * halo_high[par, s], flux], axis=0)
            block = folded(dot(side_by_side(block), weights[s]))
            lows.append(block[:width])
            highs.append(block[width:2 * width])
            endo_flux.append(block[2 * width:])
            flux = (DT * COUPLING[s]) * (arrived(0, s) - picked[3 + s])
            gap = DT * MUSC_GAP[s]
            span = pl.ds(s * length, length)
            block = jnp.concatenate(
                [gap * edge_left[par, span, :], gap * edge_right[par, span, :], flux], axis=0
            )
            block = folded(dot(side_by_side(block), weights[3 + s]))
            lefts.append(block[:length])
            rights.append(block[length:2 * length])
            musc_flux.append(block[2 * length:])

        for state, put, flux in ((endo, put_e, endo_flux), (musc, put_m, musc_flux)):
            stacked = jnp.concatenate(halves(jnp.concatenate(flux, axis=1)), axis=0)
            gain = dot(put[...], stacked)
            for s in range(3):
                state[nxt, s] = state[nxt, s] + gain[:, s * points:(s + 1) * points]
        for s in range(3):
            endo[nxt, s, pl.ds(0, width), :] += lows[s]
            endo[nxt, s, pl.ds(rows - width, width), :] += highs[s]
            first = pl.ds(0, length, stride=cycle)
            last = pl.ds(cycle - 1, length, stride=cycle)
            musc[nxt, s, first, :] = musc[nxt, s, first, :] + lefts[s]
            musc[nxt, s, last, :] = musc[nxt, s, last, :] + rights[s]

        every.wait_send()
        to_left.wait_send()
        to_right.wait_send()

        @pl.when(ax > 0)
        def _():
            low.wait_send()

        @pl.when(ax < n_ax - 1)
        def _():
            high.wait_send()

        return carry

    lax.fori_loop(0, TIME_STEPS, step, 0)
    final = TIME_STEPS % 2
    store_e = pltpu.make_async_copy(endo.at[final], endo_out, in_sems.at[0])
    store_m = pltpu.make_async_copy(musc.at[final], musc_out, in_sems.at[1])
    store_e.start()
    store_m.start()
    store_e.wait()
    store_m.wait()


def local(
    n_ax, n_circ,
    endothelium, muscle, agonist, proj_cell, proj_target, proj_count, endo_inverse, muscle_inverse
):
    n = n_ax * n_circ
    species, endo_ax, width, points = endothelium.shape
    length, cycle = muscle.shape[1:3]
    rows = endo_ax * width
    musc_rows = length * cycle
    slots = proj_cell.shape[2]
    live = jnp.arange(slots, dtype=jnp.int32)[None, :] < proj_count[0][:, None]
    marked = jnp.where(live, proj_target[0], musc_rows)
    arrived = lax.all_to_all(marked, ("ax", "circ"), split_axis=0, concat_axis=0, tiled=True)
    endo_ids = jnp.where(live, proj_cell[0], rows).T.reshape(-1)
    musc_ids = arrived.T.reshape(-1)
    vmem = pl.BlockSpec(memory_space=pltpu.VMEM)
    anywhere = pl.BlockSpec(memory_space=pl.ANY)
    dma = pltpu.SemaphoreType.DMA
    body = functools.partial(kernel, (n_ax, n_circ, width, length, cycle))
    endo_next, musc_next = pl.pallas_call(
        body,
        out_shape=(
            jax.ShapeDtypeStruct((species, rows, points), F32),
            jax.ShapeDtypeStruct((species, musc_rows, points), F32),
        ),
        in_specs=[anywhere, anywhere] + [vmem] * 7,
        out_specs=(anywhere, anywhere),
        scratch_shapes=[
            pltpu.VMEM((2, species, rows, points), F32),
            pltpu.VMEM((2, species, musc_rows, points), F32),
            pltpu.VMEM((2, species, width, points), F32),
            pltpu.VMEM((2, species, width, points), F32),
            pltpu.VMEM((2, species * length, points), F32),
            pltpu.VMEM((2, species * length, points), F32),
            pltpu.VMEM((2, species * length, points), F32),
            pltpu.VMEM((n, 16, points), F32),
            pltpu.VMEM((2, n, 16, points), F32),
            pltpu.VMEM((6, slots * n, points), F32),
            pltpu.VMEM((6, 2 * points, 2 * points), BF16),
            pltpu.VMEM((slots * n, rows), BF16),
            pltpu.VMEM((slots * n, musc_rows), BF16),
            pltpu.VMEM((rows, 2 * slots * n), BF16),
            pltpu.VMEM((musc_rows, 2 * slots * n), BF16),
            pltpu.VMEM((6, max(rows, musc_rows), 2 * points), BF16),
            dma((2,)), dma, dma, dma((2,)),
            dma((2,)), dma((2, 2)), dma((2,)), dma((2, 2)),
        ],
        compiler_params=pltpu.CompilerParams(
            collective_id=0, has_side_effects=True, vmem_limit_bytes=48 * 1024 * 1024
        ),
        name="cable_steps",
    )(
        endothelium.reshape(species, rows, points),
        muscle.reshape(species, musc_rows, points),
        agonist.reshape(rows, points),
        endo_ids[:, None], jnp.tile(endo_ids, 2)[None, :],
        musc_ids[:, None], jnp.tile(musc_ids, 2)[None, :],
        endo_inverse, muscle_inverse,
    )
    return endo_next.reshape(endothelium.shape), musc_next.reshape(muscle.shape)


def solution(mesh):
    tiles = P(None, "ax", "circ", None)
    sent = P(("ax", "circ"), None, None)
    return jax.shard_map(
        functools.partial(local, mesh.shape["ax"], mesh.shape["circ"]),
        mesh=mesh,
        in_specs=(tiles, tiles, P("ax", "circ", None), sent, sent, P(("ax", "circ"), None), P(), P()),
        out_specs=(tiles, tiles),
        check_vma=False,
    )
```

profile of v0, /device:TPU:1, one launch (start us, length us, event | category | flops | bytes accessed | tf_op | source)
XLA Modules:
  0.0 103.1 jit_solution(6938445493089177053)
XLA Ops:
  0.6 0.0 copy-start.5
  0.6 0.0 copy-start.6
  0.6 0.6 copy-done.5
  1.3 0.0 copy-done.6
  1.3 0.7 copy.12
  2.0 0.0 copy-start.7
  2.0 7.1 %all-to-all-start = ((s32[32,1,2]{2,1,0:T(1,128)}), s32[32,1,2]{2,1,0:T(1,128)S(1)}, u32[]{:S(2)}, u32[]{:S(2)}) async-start(s32[32,1,2]{2,1,0:T(1,128)} %copy.12), calls=%async_computation | async-start | bytes 32768 | tf_op jit(solution)/shard_map/all_to_all | solution.py:303
  9.1 0.0 copy-done.7
  9.2 0.1 tile.14
  9.2 0.1 broadcast_in_dim_reshape.8.endo_col
  9.4 0.1 broadcast_in_dim_tile.6.endo_row
  9.4 6.3 %all-to-all-done = s32[32,1,2]{2,1,0:T(1,128)S(1)} async-done(((s32[32,1,2]{2,1,0:T(1,128)}), s32[32,1,2]{2,1,0:T(1,128)S(1)}, u32[]{:S(2)}, u32[]{:S(2)}) %all-to-all-start) | async-done | bytes 288 | tf_op jit(solution)/shard_map/all_to_all | solution.py:303
  15.7 0.1 copy.13
  15.8 0.1 tile.16
  15.9 0.1 broadcast_in_dim_reshape.9.musc_col
  16.0 0.1 broadcast_in_dim_tile.7.musc_row
  16.1 1.1 %copy-done = f32[3,4,128,128]{3,2,1,0:T(8,128)S(1)} copy-done((f32[3,4,128,128]{3,2,1,0:T(8,128)S(1)}, f32[3,4,128,128]{3,2,1,0:T(8,128)}, u32[]{:S(2)}) %copy-start) | copy-done | bytes 786456
  17.2 1.1 %copy-done.1 = f32[3,8,64,128]{3,2,1,0:T(8,128)S(1)} copy-done((f32[3,8,64,128]{3,2,1,0:T(8,128)S(1)}, f32[3,8,64,128]{3,2,1,0:T(8,128)}, u32[]{:S(2)}) %copy-start.1) | copy-done | bytes 786456
  18.4 0.9 copy-done.2
  19.3 0.9 copy-done.3
  20.3 0.9 copy-done.4
  21.2 80.1 %cable_steps.1 = (f32[3,512,128]{2,1,0:T(8,128)S(1)}, f32[3,512,128]{2,1,0:T(8,128)S(1)}) custom-call(f32[3,512,128]{2,1,0:T(8,128)S(1)} %bitcast.17, f32[3,512,128]{2,1,0:T(8,128)S(1)} %bitcast.18, f32[512,128]{1,0:T(8,128)S(1)} %bitcast.19, s32[64,1]{1,0:T(8,128)S(1)} %broadcast_in_dim_reshape.8.endo_col, s32[1,128]{1,0:T(1,128)S(1)} %broadcast_in_dim_tile.6.endo_row, ...), custom_call_target="tpu_custom_call" | custom-call | tf_op jit(solution)/shard_map/cable_steps/pallas_call | solution.py:310
  101.3 0.9 copy.18
  102.2 0.9 copy.19
  (9 shorter events, 0.0 us)
Async XLA Ops:
  0.6 0.7 copy-start.5
  0.6 0.7 copy-start.6
  2.0 7.1 %copy-start.7 = (s32[1,32,2]{1,2,0:T(2,128)S(1)}, s32[1,32,2]{1,2,0:T(2,128)}, u32[]{:S(2)}) copy-start(s32[1,32,2]{1,2,0:T(2,128)} %param.11) | copy-start | bytes 772
  2.0 13.7 %all-to-all-start = ((s32[32,1,2]{2,1,0:T(1,128)}), s32[32,1,2]{2,1,0:T(1,128)S(1)}, u32[]{:S(2)}, u32[]{:S(2)}) async-start(s32[32,1,2]{2,1,0:T(1,128)} %copy.12), calls=%async_computation | async-start | bytes 32768 | tf_op jit(solution)/shard_map/all_to_all | solution.py:303
  16.1 1.1 %copy-start = (f32[3,4,128,128]{3,2,1,0:T(8,128)S(1)}, f32[3,4,128,128]{3,2,1,0:T(8,128)}, u32[]{:S(2)}) copy-start(f32[3,4,128,128]{3,2,1,0:T(8,128)} %param.8) | copy-start | bytes 2359300
  17.2 1.1 %copy-start.1 = (f32[3,8,64,128]{3,2,1,0:T(8,128)S(1)}, f32[3,8,64,128]{3,2,1,0:T(8,128)}, u32[]{:S(2)}) copy-start(f32[3,8,64,128]{3,2,1,0:T(8,128)} %param.9) | copy-start | bytes 2359300
  18.4 0.9 copy-start.2
  19.3 0.9 copy-start.3
  20.3 0.9 copy-start.4
where the time goes:
time: 104 us; the launch traced here: 103 us
  Pallas kernels  80.1 us (77%)
  local copies, waits for them, and re-layouts  8.82 us (8%)
  starting transfers between devices  7.1 us (7%)
  waiting for transfers between devices  6.31 us (6%)
    pallas_call x1, Pallas kernels, local(): pl.pallas_call(body, out_shape=(jax.ShapeDtypeStruct((species, rows, poin...  80.1 us
    unnamed x18, local copies, waits for them, and re-layouts  7.51 us
    all_to_all x1, starting transfers between devices, local(): lax.all_to_all(marked, ('ax', 'circ'), split_axis=0, concat_axis=0, tiled...  7.1 us
    all_to_all x1, waiting for transfers between devices, local(): lax.all_to_all(marked, ('ax', 'circ'), split_axis=0, concat_axis=0, tiled...  6.31 us
  transfers between devices with their start and end apart: 1, of which 1 were waited for; matrix products, arithmetic and copies ran while one was open for 0% of the time, Pallas kernels for 0%

commit v1 on v0

v1 whole, which is shorter than its diff:
```python
import functools

import jax
import jax.numpy as jnp
from jax import lax
from jax.experimental import pallas as pl
from jax.experimental.pallas import tpu as pltpu
from jax.sharding import PartitionSpec as P

MESH = pl.DeviceIdType.MESH
TIME_STEPS = 8
DT = 0.2
COUPLING = (0.1, 0.3, 0.5)
ENDO_GAP = (0.05, 0.3, 0.5)
MUSC_GAP = (0.05, 0.1, 0.4)
BF16 = jnp.bfloat16
F32 = jnp.float32


def halves(x):
    high = x.astype(BF16)
    return high, (x - high.astype(F32)).astype(BF16)


def side_by_side(x):
    return jnp.concatenate(halves(x), axis=1)


def folded(y):
    half = y.shape[1] // 2
    return y[:, :half] + y[:, half:]


def dot(a, b):
    return jnp.dot(a, b, preferred_element_type=F32)


def reaction(u0, u1, u2, drive):
    square = u1 * u1
    release = square / (0.5 + square)
    second = -0.5 * u1 if drive is None else drive - 0.5 * u1
    return (1.2 * release - 0.6 * u0 - 0.2 * u2, second, 0.5 * u0 - 0.8 * u2)


def kernel(
    sizes,
    endo_in, musc_in, agonist_in, meta_in, endo_inv_in, musc_inv_in,
    endo_out, musc_out,
    endo, musc, halo_low, halo_high, edge_out, edge_left, edge_right,
    send, recv, picked, base_rows, weights, take_e, take_m, put_e, put_m, mix_e, mix_m, rhs,
    block_e, block_m, agonist, meta, meta_recv, endo_inv, musc_inv,
    in_sems, own_sem, send_sem, recv_sem, halo_send, halo_recv, edge_send, edge_recv,
    meta_sems,
):
    n_ax, n_circ, width, length, cycle = sizes
    n = n_ax * n_circ
    points = endo.shape[3]
    rows = endo.shape[2]
    musc_rows = musc.shape[2]
    ax = lax.axis_index("ax")
    circ = lax.axis_index("circ")
    me = ax * n_circ + circ
    right = lax.rem(circ + 1, n_circ)
    left = lax.rem(circ + n_circ - 1, n_circ)
    turned = [lax.rem(circ + c, n_circ) for c in range(n_circ)]

    def each_peer(act):
        def some(j, carry):
            far = lax.rem(ax + j, n_ax)
            for c in reversed(range(n_circ)):
                act(far, turned[c])
            return carry

        lax.fori_loop(1, n_ax, some, 0)
        for c in reversed(range(1, n_circ)):
            act(ax, turned[c])

    loads = [
        pltpu.make_async_copy(a, b, in_sems.at[i])
        for i, (a, b) in enumerate(
            (
                (meta_in, meta), (endo_in, endo.at[0]), (musc_in, musc.at[0]),
                (endo_inv_in, endo_inv), (musc_inv_in, musc_inv), (agonist_in, agonist),
            )
        )
    ]
    for load in loads:
        load.start()

    barrier = pltpu.get_barrier_semaphore()

    def greet(pa, pc):
        pl.semaphore_signal(barrier, inc=1, device_id=(pa, pc), device_id_type=MESH)

    each_peer(greet)

    @pl.when(ax == 0)
    def _():
        halo_low[...] = jnp.zeros_like(halo_low)

    @pl.when(ax == n_ax - 1)
    def _():
        halo_high[...] = jnp.zeros_like(halo_high)

    for load in loads:
        load.wait()
    pl.semaphore_wait(barrier, n - 1)

    def tell(pa, pc):
        pltpu.make_async_remote_copy(
            src_ref=meta.at[pa * n_circ + pc], dst_ref=meta_recv.at[me],
            send_sem=meta_sems.at[0], recv_sem=meta_sems.at[1],
            device_id=(pa, pc), device_id_type=MESH,
        ).start()

    each_peer(tell)
    own_meta = pltpu.make_async_copy(meta.at[me], meta_recv.at[me], own_sem)
    own_meta.start()

    for layer, inv in ((0, endo_inv), (1, musc_inv)):
        for s in range(3):
            row = side_by_side(inv[s].T)
            weights[layer * 3 + s] = jnp.concatenate([row, row], axis=0)

    def choose(ids, take, put):
        cells = lax.broadcasted_iota(jnp.int32, take.shape, 1)
        chosen = jnp.where(cells == ids, 1.0, 0.0)
        take[...] = chosen.astype(BF16)
        spread = chosen.T
        put[...] = jnp.concatenate([spread, spread], axis=1).astype(BF16)
        return chosen, dot(chosen.astype(BF16), spread.astype(BF16))

    sent = meta[:, 0, :]
    ids = jnp.concatenate([sent[:, 2:3], sent[:, 3:4]], axis=0)
    chosen, same = choose(ids, take_e, put_e)
    mix_e[...] = jnp.concatenate(
        [chosen[:, :width], chosen[:, rows - width:], same], axis=1
    ).astype(BF16)

    def gather(layer, s, values, out):
        take = take_e if layer == 0 else take_m
        out[layer * 3 + s] = folded(dot(take[...], side_by_side(values)))

    for s in range(3):
        gather(0, s, endo[0, s], picked)

    told = pltpu.make_async_remote_copy(
        src_ref=meta.at[pl.ds(0, n - 1)], dst_ref=meta_recv.at[pl.ds(0, n - 1)],
        send_sem=meta_sems.at[0], recv_sem=meta_sems.at[1],
        device_id=(ax, right), device_id_type=MESH,
    )
    told.wait_recv()
    own_meta.wait()
    got = meta_recv[:, 0, :]
    ids = jnp.concatenate([got[:, 0:1], got[:, 1:2]], axis=0)
    chosen, same = choose(ids, take_m, put_m)
    starts = lax.broadcasted_iota(jnp.int32, (ids.shape[0], length), 1) * cycle
    mix_m[...] = jnp.concatenate(
        [
            jnp.where(starts == ids, 1.0, 0.0),
            jnp.where(starts + (cycle - 1) == ids, 1.0, 0.0),
            same,
        ],
        axis=1,
    ).astype(BF16)
    for s in range(3):
        gather(1, s, musc[0, s], picked)
    told.wait_send()

    def messages(par):
        return pltpu.make_async_remote_copy(
            src_ref=send.at[par, pl.ds(0, n - 1), pl.ds(0, 12)],
            dst_ref=recv.at[par, pl.ds(0, n - 1), pl.ds(0, 12)],
            send_sem=send_sem.at[par], recv_sem=recv_sem.at[par],
            device_id=(ax, right), device_id_type=MESH,
        )

    def own_copy(par):
        return pltpu.make_async_copy(
            send.at[par, me, pl.ds(0, 12)], recv.at[par, me, pl.ds(0, 12)], own_sem
        )

    def pack(par):
        flat = send.at[par].reshape(n * 16, points)
        for q in range(6):
            for slot in range(2):
                flat[pl.ds(q * 2 + slot, n, stride=16), :] = picked[q, pl.ds(slot * n, n), :]

    def launch(par):
        def post(pa, pc):
            pltpu.make_async_remote_copy(
                src_ref=send.at[par, pa * n_circ + pc, pl.ds(0, 12)],
                dst_ref=recv.at[par, me, pl.ds(0, 12)],
                send_sem=send_sem.at[par],
                recv_sem=recv_sem.at[par],
                device_id=(pa, pc),
                device_id_type=MESH,
            ).start()

        each_peer(post)
        own_copy(par).start()

    def ends(par):
        low = pltpu.make_async_remote_copy(
            src_ref=endo.at[par, :, pl.ds(0, width)], dst_ref=halo_high.at[par],
            send_sem=halo_send.at[0], recv_sem=halo_recv.at[par, 0],
            device_id=(ax - 1, circ), device_id_type=MESH,
        )
        high = pltpu.make_async_remote_copy(
            src_ref=endo.at[par, :, pl.ds(rows - width, width)], dst_ref=halo_low.at[par],
            send_sem=halo_send.at[1], recv_sem=halo_recv.at[par, 1],
            device_id=(ax + 1, circ), device_id_type=MESH,
        )
        return low, high

    def sides(par):
        to_left = pltpu.make_async_remote_copy(
            src_ref=edge_out.at[0], dst_ref=edge_right.at[par],
            send_sem=edge_send.at[0], recv_sem=edge_recv.at[par, 0],
            device_id=(ax, left), device_id_type=MESH,
        )
        to_right = pltpu.make_async_remote_copy(
            src_ref=edge_out.at[1], dst_ref=edge_left.at[par],
            send_sem=edge_send.at[1], recv_sem=edge_recv.at[par, 1],
            device_id=(ax, right), device_id_type=MESH,
        )
        return to_left, to_right

    def start_ends(par):
        low, high = ends(par)
        pl.when(ax > 0)(low.start)
        pl.when(ax < n_ax - 1)(high.start)

    def start_sides(par):
        for s in range(3):
            span = pl.ds(s * length, length)
            edge_out[0, span] = musc[par, s, pl.ds(0, length, stride=cycle), :]
            edge_out[1, span] = musc[par, s, pl.ds(cycle - 1, length, stride=cycle), :]
        for copy in sides(par):
            copy.start()

    def local_part(par, nxt, last):
        count = rows // width
        for a in range(count):
            for j in range(0, width, 64):
                here = pl.ds(a * width + j, 64)
                u = [endo[par, s, here, :] for s in range(3)]
                parts = reaction(u[0], u[1], u[2], agonist[here, :])
                for s in range(3):
                    lap = -2.0 * u[s]
                    if a > 0:
                        lap = lap + endo[par, s, pl.ds((a - 1) * width + j, 64), :]
                    if a < count - 1:
                        lap = lap + endo[par, s, pl.ds((a + 1) * width + j, 64), :]
                    value = u[s] + DT * (parts[s] + ENDO_GAP[s] * lap)
                    rhs[s, here, :] = side_by_side(value)

        def musc_base(a, carry):
            here = pl.ds(pl.multiple_of(a * cycle, cycle), cycle)
            place_in = lax.broadcasted_iota(jnp.int32, (cycle, points), 0)
            u = [musc[par, s, here, :] for s in range(3)]
            parts = reaction(u[0], u[1], u[2], None)
            for s in range(3):
                before = jnp.where(place_in == 0, 0.0, pltpu.roll(u[s], 1, 0))
                after = jnp.where(place_in == cycle - 1, 0.0, pltpu.roll(u[s], cycle - 1, 0))
                lap = before + after - 2.0 * u[s]
                value = u[s] + DT * (parts[s] + MUSC_GAP[s] * lap)
                rhs[3 + s, here, :] = side_by_side(value)
            return carry

        lax.fori_loop(0, length, musc_base, 0)

        for layer, state in ((0, endo), (1, musc)):
            for s in range(3):
                value = folded(dot(rhs[layer * 3 + s], weights[layer * 3 + s]))
                state[nxt, s] = value
                if not last:
                    gather(layer, s, value, base_rows)

    def collect(par):
        own_copy(par).wait()
        messages(par).wait_recv()
        for copy in sides(par):
            copy.wait()
        low, high = ends(par)

        @pl.when(ax > 0)
        def _():
            low.wait_send()
            high.wait_recv()

        @pl.when(ax < n_ax - 1)
        def _():
            high.wait_send()
            low.wait_recv()

    def arrived(par, layer, s):
        flat = recv.at[par].reshape(n * 16, points)
        k = layer * 6 + s * 2
        return jnp.concatenate(
            [flat[pl.ds(k + slot, n, stride=16), :] for slot in range(2)], axis=0
        )

    def from_outside(par, last):
        for s in range(3):
            flux = (DT * COUPLING[s]) * (arrived(par, 1, s) - picked[s])
            gap = DT * ENDO_GAP[s]
            value = jnp.concatenate([gap * halo_low[par, s], gap * halo_high[par, s], flux], axis=0)
            value = folded(dot(side_by_side(value), weights[s]))
            block_e[s] = value
            fresh_e = None if last else base_rows[s] + folded(dot(mix_e[...], side_by_side(value)))
            flux = (DT * COUPLING[s]) * (arrived(par, 0, s) - picked[3 + s])
            gap = DT * MUSC_GAP[s]
            span = pl.ds(s * length, length)
            value = jnp.concatenate(
                [gap * edge_left[par, span, :], gap * edge_right[par, span, :], flux], axis=0
            )
            value = folded(dot(side_by_side(value), weights[3 + s]))
            block_m[s] = value
            if not last:
                picked[s] = fresh_e
                picked[3 + s] = base_rows[3 + s] + folded(dot(mix_m[...], side_by_side(value)))

    def finish_endo(nxt):
        flux = jnp.concatenate([block_e[s, pl.ds(2 * width, 2 * n), :] for s in range(3)], axis=1)
        gain = dot(put_e[...], jnp.concatenate(halves(flux), axis=0))
        for s in range(3):
            endo[nxt, s] += gain[:, s * points:(s + 1) * points]
            endo[nxt, s, pl.ds(0, width), :] += block_e[s, pl.ds(0, width), :]
            endo[nxt, s, pl.ds(rows - width, width), :] += block_e[s, pl.ds(width, width), :]

    def finish_musc(nxt):
        flux = jnp.concatenate([block_m[s, pl.ds(2 * length, 2 * n), :] for s in range(3)], axis=1)
        gain = dot(put_m[...], jnp.concatenate(halves(flux), axis=0))
        first = pl.ds(0, length, stride=cycle)
        final = pl.ds(cycle - 1, length, stride=cycle)
        for s in range(3):
            musc[nxt, s] += gain[:, s * points:(s + 1) * points]
            musc[nxt, s, first, :] = musc[nxt, s, first, :] + block_m[s, pl.ds(0, length), :]
            musc[nxt, s, final, :] = musc[nxt, s, final, :] + block_m[s, pl.ds(length, length), :]

    pack(0)
    launch(0)
    start_ends(0)
    start_sides(0)

    def step(t, carry):
        par = lax.rem(t, 2)
        nxt = 1 - par
        local_part(par, nxt, False)
        collect(par)
        from_outside(par, False)
        pl.when(t > 0)(lambda: messages(nxt).wait_send())
        pack(nxt)
        launch(nxt)
        finish_endo(nxt)
        start_ends(nxt)
        finish_musc(nxt)
        start_sides(nxt)
        return carry

    lax.fori_loop(0, TIME_STEPS - 1, step, 0)
    par = (TIME_STEPS - 1) % 2
    nxt = 1 - par
    local_part(par, nxt, True)
    collect(par)
    from_outside(par, True)
    finish_endo(nxt)
    store_e = pltpu.make_async_copy(endo.at[nxt], endo_out, in_sems.at[0])
    store_e.start()
    finish_musc(nxt)
    store_m = pltpu.make_async_copy(musc.at[nxt], musc_out, in_sems.at[1])
    store_m.start()
    messages(nxt).wait_send()
    messages(par).wait_send()
    store_e.wait()
    store_m.wait()


def local(
    n_ax, n_circ,
    endothelium, muscle, agonist, proj_cell, proj_target, proj_count, endo_inverse, muscle_inverse
):
    n = n_ax * n_circ
    species, endo_ax, width, points = endothelium.shape
    length, cycle = muscle.shape[1:3]
    rows = endo_ax * width
    musc_rows = length * cycle
    slots = proj_cell.shape[2]
    lane = jnp.arange(points, dtype=jnp.int32)[None, :]
    target, cell = proj_target[0], proj_cell[0]
    live = lane % slots < proj_count[0][:, None]
    first = jnp.where(lane == 0, target[:, 0:1], target[:, 1:2])
    second = jnp.where(lane == slots, cell[:, 0:1], cell[:, 1:2])
    meta = jnp.where(live, jnp.where(lane < slots, first, second), rows + musc_rows)
    anywhere = pl.BlockSpec(memory_space=pl.ANY)
    dma = pltpu.SemaphoreType.DMA
    body = functools.partial(kernel, (n_ax, n_circ, width, length, cycle))
    endo_next, musc_next = pl.pallas_call(
        body,
        out_shape=(
            jax.ShapeDtypeStruct((species, rows, points), F32),
            jax.ShapeDtypeStruct((species, musc_rows, points), F32),
        ),
        in_specs=[anywhere] * 6,
        out_specs=(anywhere, anywhere),
        scratch_shapes=[
            pltpu.VMEM((2, species, rows, points), F32),
            pltpu.VMEM((2, species, musc_rows, points), F32),
            pltpu.VMEM((2, species, width, points), F32),
            pltpu.VMEM((2, species, width, points), F32),
            pltpu.VMEM((2, species * length, points), F32),
            pltpu.VMEM((2, species * length, points), F32),
            pltpu.VMEM((2, species * length, points), F32),
            pltpu.VMEM((2, n, 16, points), F32),
            pltpu.VMEM((2, n, 16, points), F32),
            pltpu.VMEM((6, slots * n, points), F32),
            pltpu.VMEM((6, slots * n, points), F32),
            pltpu.VMEM((6, 2 * points, 2 * points), BF16),
            pltpu.VMEM((slots * n, rows), BF16),
            pltpu.VMEM((slots * n, musc_rows), BF16),
            pltpu.VMEM((rows, 2 * slots * n), BF16),
            pltpu.VMEM((musc_rows, 2 * slots * n), BF16),
            pltpu.VMEM((slots * n, 2 * width + slots * n), BF16),
            pltpu.VMEM((slots * n, 2 * length + slots * n), BF16),
            pltpu.VMEM((6, max(rows, musc_rows), 2 * points), BF16),
            pltpu.VMEM((species, 2 * width + slots * n, points), F32),
            pltpu.VMEM((species, 2 * length + slots * n, points), F32),
            pltpu.VMEM((rows, points), F32),
            pltpu.VMEM((n, 1, points), jnp.int32),
            pltpu.VMEM((n, 1, points), jnp.int32),
            pltpu.VMEM((species, points, points), F32),
            pltpu.VMEM((species, points, points), F32),
            dma((6,)), dma, dma((2,)), dma((2,)),
            dma((2,)), dma((2, 2)), dma((2,)), dma((2, 2)),
            dma((2,)),
        ],
        compiler_params=pltpu.CompilerParams(
            collective_id=0, has_side_effects=True, vmem_limit_bytes=60 * 1024 * 1024
        ),
        name="cable_steps",
    )(
        endothelium.reshape(species, rows, points),
        muscle.reshape(species, musc_rows, points),
        agonist.reshape(rows, points),
        meta[:, None, :],
        endo_inverse, muscle_inverse,
    )
    return endo_next.reshape(endothelium.shape), musc_next.reshape(muscle.shape)


def solution(mesh):
    tiles = P(None, "ax", "circ", None)
    sent = P(("ax", "circ"), None, None)
    return jax.shard_map(
        functools.partial(local, mesh.shape["ax"], mesh.shape["circ"]),
        mesh=mesh,
        in_specs=(tiles, tiles, P("ax", "circ", None), sent, sent, P(("ax", "circ"), None), P(), P()),
        out_specs=(tiles, tiles),
        check_vma=False,
    )
```

time: 104 us -> 86.8 us (0.83)
  starting transfers between devices: 7.1 us -> 0 us
  waiting for transfers between devices: 6.31 us -> 0 us
  local copies, waits for them, and re-layouts: 8.82 us -> 4.36 us
    all_to_all x1 -> x0, starting transfers between devices: 7.1 us -> none  [local(): lax.all_to_all(marked, ('ax', 'circ'), split_axis=0, concat_axis=0, tiled...]
    all_to_all x1 -> x0, waiting for transfers between devices: 6.31 us -> none  [local(): lax.all_to_all(marked, ('ax', 'circ'), split_axis=0, concat_axis=0, tiled...]
    unnamed x18 -> x10, local copies, waits for them, and re-layouts: 7.51 us -> 4.36 us
  transfers between devices with their start and end apart: 1 -> 0, of which waited for: 1 -> 0; matrix products, arithmetic and copies ran while one was open for 0% -> 0% of each run, Pallas kernels for 0% -> 0%
where the time goes in v1:
time: 86.8 us; the launch traced here: 86.5 us
  Pallas kernels  80.6 us (93%)
  local copies, waits for them, and re-layouts  4.36 us (5%)
    pallas_call x1, Pallas kernels, local(): pl.pallas_call(body, out_shape=(jax.ShapeDtypeStruct((species, rows, poin...  80.6 us
    unnamed x10, local copies, waits for them, and re-layouts  4.36 us

profile of v1, /device:TPU:1, one launch (start us, length us, event | category | flops | bytes accessed | tf_op | source)
XLA Modules:
  0.0 86.5 jit_solution(14699036173317783772)
XLA Ops:
  0.7 0.0 copy-start.2
  0.7 0.0 copy-start.1
  0.7 0.7 copy-done.2
  1.3 0.0 copy-done.1
  1.4 0.0 copy-start.3
  1.4 0.7 copy-done.3
  2.0 0.8 compare_select_fusion.meta_in
  2.9 80.6 %cable_steps.1 = (f32[3,512,128]{2,1,0:T(8,128)}, f32[3,512,128]{2,1,0:T(8,128)}) custom-call(f32[3,512,128]{2,1,0:T(8,128)} %bitcast.16, f32[3,512,128]{2,1,0:T(8,128)} %bitcast.17, f32[512,128]{1,0:T(8,128)} %bitcast.20, s32[32,1,128]{2,1,0:T(1,128)} %compare_select_fusion.meta_in, f32[3,128,128]{2,1,0:T(8,128)} %endo_inv_in.1, f32[3,128,128]{2,1,0:T(8,128)} %musc_inv_in.1), custom_call_target="tpu_custom_call" | custom-call | tf_op jit(solution)/shard_map/cable_steps/pallas_call | solution.py:399
  83.5 0.0 copy-start
  83.5 2.1 %copy.12 = f32[3,4,128,128]{3,2,1,0:T(8,128)} copy(f32[3,4,128,128]{3,2,1,0:T(8,128)} %bitcast.19) | data formatting | bytes 1572864
  85.7 0.0 copy-done
  85.7 0.9 %copy.13 = f32[3,8,64,128]{3,2,1,0:T(8,128)} copy(f32[3,8,64,128]{3,2,1,0:T(8,128)S(1)} %bitcast.18) | data formatting | bytes 1572864
  (4 shorter events, 0.0 us)
Async XLA Ops:
  0.7 0.7 copy-start.2
  0.7 0.7 copy-start.1
  1.4 0.7 copy-start.3
  83.5 2.1 %copy-start = (f32[3,512,128]{2,1,0:T(8,128)S(1)}, f32[3,512,128]{2,1,0:T(8,128)}, u32[]{:S(2)}) copy-start(f32[3,512,128]{2,1,0:T(8,128)} %get-tuple-element.5) | copy-start | bytes 2359300

commit v2 on v1

--- a/solution.py
+++ b/solution.py
@@ -50,7 +50,7 @@
     send, recv, picked, base_rows, weights, take_e, take_m, put_e, put_m, mix_e, mix_m, rhs,
     block_e, block_m, agonist, meta, meta_recv, endo_inv, musc_inv,
     in_sems, own_sem, send_sem, recv_sem, halo_send, halo_recv, edge_send, edge_recv,
-    meta_sems,
+    meta_sems, relay, relay_recv, relay_send,
 ):
     n_ax, n_circ, width, length, cycle = sizes
     n = n_ax * n_circ
@@ -62,6 +62,13 @@
     me = ax * n_circ + circ
     right = lax.rem(circ + 1, n_circ)
     left = lax.rem(circ + n_circ - 1, n_circ)
+    half = width // 2
+    corners = n_ax % 4 == 0 and n_ax > 4
+    turn = lax.rem(ax, 4)
+    up_far = (turn == 3) & (ax < n_ax - 1)
+    down_far = (turn == 0) & (ax > 0)
+    relay_up = (turn == 3) & (ax > 3)
+    relay_down = (turn == 0) & (ax < n_ax - 4)
     turned = [lax.rem(circ + c, n_circ) for c in range(n_circ)]
 
     def each_peer(act):
@@ -102,8 +109,7 @@
     def _():
         halo_high[...] = jnp.zeros_like(halo_high)
 
-    for load in loads:
-        load.wait()
+    loads[0].wait()
     pl.semaphore_wait(barrier, n - 1)
 
     def tell(pa, pc):
@@ -117,6 +123,8 @@
     own_meta = pltpu.make_async_copy(meta.at[me], meta_recv.at[me], own_sem)
     own_meta.start()
 
+    loads[3].wait()
+    loads[4].wait()
     for layer, inv in ((0, endo_inv), (1, musc_inv)):
         for s in range(3):
             row = side_by_side(inv[s].T)
@@ -141,6 +149,9 @@
         take = take_e if layer == 0 else take_m
         out[layer * 3 + s] = folded(dot(take[...], side_by_side(values)))
 
+    loads[1].wait()
+    loads[2].wait()
+    loads[5].wait()
     for s in range(3):
         gather(0, s, endo[0, s], picked)
 
@@ -200,18 +211,62 @@
         each_peer(post)
         own_copy(par).start()
 
-    def ends(par):
-        low = pltpu.make_async_remote_copy(
-            src_ref=endo.at[par, :, pl.ds(0, width)], dst_ref=halo_high.at[par],
-            send_sem=halo_send.at[0], recv_sem=halo_recv.at[par, 0],
-            device_id=(ax - 1, circ), device_id_type=MESH,
-        )
-        high = pltpu.make_async_remote_copy(
-            src_ref=endo.at[par, :, pl.ds(rows - width, width)], dst_ref=halo_low.at[par],
-            send_sem=halo_send.at[1], recv_sem=halo_recv.at[par, 1],
-            device_id=(ax + 1, circ), device_id_type=MESH,
-        )
-        return low, high
+    def cells(par, from_top, start, count):
+        first = rows - width if from_top else 0
+        return endo.at[par, :, pl.ds(first + start, count)]
+
+    def end_copy(par, up, start, count):
+        dst = halo_low if up else halo_high
+        return pltpu.make_async_remote_copy(
+            src_ref=cells(par, up, start, count), dst_ref=dst.at[par, :, pl.ds(start, count)],
+            send_sem=halo_send.at[int(up)], recv_sem=halo_recv.at[par, int(up)],
+            device_id=(ax + 1 if up else ax - 1, circ), device_id_type=MESH,
+        )
+
+    def to_relay(par, up):
+        return pltpu.make_async_remote_copy(
+            src_ref=cells(par, up, half, width - half), dst_ref=relay.at[par, int(up)],
+            send_sem=halo_send.at[int(up)], recv_sem=relay_recv.at[par, int(up)],
+            device_id=(ax + 4 if up else ax - 4, circ), device_id_type=MESH,
+        )
+
+    def from_relay(par, up):
+        dst = halo_low if up else halo_high
+        return pltpu.make_async_remote_copy(
+            src_ref=relay.at[par, int(up)], dst_ref=dst.at[par, :, pl.ds(half, width - half)],
+            send_sem=relay_send.at[int(up)], recv_sem=halo_recv.at[par, int(up)],
+            device_id=(ax - 3 if up else ax + 3, circ), device_id_type=MESH,
+        )
+
+    def start_far(par):
+        if corners:
+            pl.when(up_far)(to_relay(par, True).start)
+            pl.when(down_far)(to_relay(par, False).start)
+
+    def start_ends(par):
+        if corners:
+            pl.when(up_far)(end_copy(par, True, 0, half).start)
+            pl.when(down_far)(end_copy(par, False, 0, half).start)
+            pl.when((ax < n_ax - 1) & (turn != 3))(end_copy(par, True, 0, width).start)
+            pl.when((ax > 0) & (turn != 0))(end_copy(par, False, 0, width).start)
+        else:
+            pl.when(ax < n_ax - 1)(end_copy(par, True, 0, width).start)
+            pl.when(ax > 0)(end_copy(par, False, 0, width).start)
+
+    def pass_on(par):
+        if not corners:
+            return
+        for up, here in ((True, relay_up), (False, relay_down)):
+
+            @pl.when(here)
+            def _():
+                to_relay(par, up).wait_recv()
+                from_relay(par, up).start()
+
+    def passed_on(par):
+        if corners:
+            pl.when(relay_up)(from_relay(par, True).wait_send)
+            pl.when(relay_down)(from_relay(par, False).wait_send)
 
     def sides(par):
         to_left = pltpu.make_async_remote_copy(
@@ -225,11 +280,6 @@
             device_id=(ax, right), device_id_type=MESH,
         )
         return to_left, to_right
-
-    def start_ends(par):
-        low, high = ends(par)
-        pl.when(ax > 0)(low.start)
-        pl.when(ax < n_ax - 1)(high.start)
 
     def start_sides(par):
         for s in range(3):
@@ -269,6 +319,7 @@
             return carry
 
         lax.fori_loop(0, length, musc_base, 0)
+        pass_on(par)
 
         for layer, state in ((0, endo), (1, musc)):
             for s in range(3):
@@ -282,17 +333,17 @@
         messages(par).wait_recv()
         for copy in sides(par):
             copy.wait()
-        low, high = ends(par)
+        passed_on(par)
 
         @pl.when(ax > 0)
         def _():
-            low.wait_send()
-            high.wait_recv()
+            end_copy(par, False, 0, width).wait_send()
+            end_copy(par, True, 0, width).wait_recv()
 
         @pl.when(ax < n_ax - 1)
         def _():
-            high.wait_send()
-            low.wait_recv()
+            end_copy(par, True, 0, width).wait_send()
+            end_copy(par, False, 0, width).wait_recv()
 
     def arrived(par, layer, s):
         flat = recv.at[par].reshape(n * 16, points)
@@ -301,33 +352,47 @@
             [flat[pl.ds(k + slot, n, stride=16), :] for slot in range(2)], axis=0
         )
 
-    def from_outside(par, last):
+    def endo_outside(par):
         for s in range(3):
             flux = (DT * COUPLING[s]) * (arrived(par, 1, s) - picked[s])
             gap = DT * ENDO_GAP[s]
             value = jnp.concatenate([gap * halo_low[par, s], gap * halo_high[par, s], flux], axis=0)
-            value = folded(dot(side_by_side(value), weights[s]))
-            block_e[s] = value
-            fresh_e = None if last else base_rows[s] + folded(dot(mix_e[...], side_by_side(value)))
+            block_e[s] = folded(dot(side_by_side(value), weights[s]))
+
+    def musc_outside(par):
+        for s in range(3):
             flux = (DT * COUPLING[s]) * (arrived(par, 0, s) - picked[3 + s])
             gap = DT * MUSC_GAP[s]
             span = pl.ds(s * length, length)
             value = jnp.concatenate(
                 [gap * edge_left[par, span, :], gap * edge_right[par, span, :], flux], axis=0
             )
-            value = folded(dot(side_by_side(value), weights[3 + s]))
-            block_m[s] = value
-            if not last:
-                picked[s] = fresh_e
-                picked[3 + s] = base_rows[3 + s] + folded(dot(mix_m[...], side_by_side(value)))
-
-    def finish_endo(nxt):
+            block_m[s] = folded(dot(side_by_side(value), weights[3 + s]))
+
+    def pick():
+        for s in range(3):
+            picked[s] = base_rows[s] + folded(dot(mix_e[...], side_by_side(block_e[s])))
+            picked[3 + s] = base_rows[3 + s] + folded(dot(mix_m[...], side_by_side(block_m[s])))
+
+    def endo_flux():
         flux = jnp.concatenate([block_e[s, pl.ds(2 * width, 2 * n), :] for s in range(3)], axis=1)
-        gain = dot(put_e[...], jnp.concatenate(halves(flux), axis=0))
-        for s in range(3):
-            endo[nxt, s] += gain[:, s * points:(s + 1) * points]
-            endo[nxt, s, pl.ds(0, width), :] += block_e[s, pl.ds(0, width), :]
-            endo[nxt, s, pl.ds(rows - width, width), :] += block_e[s, pl.ds(width, width), :]
+        return jnp.concatenate(halves(flux), axis=0)
+
+    def finish_ends(nxt):
+        flux = endo_flux()
+        for i, first in enumerate((0, rows - width)):
+            span = pl.ds(first, width)
+            gain = dot(put_e[span, :], flux)
+            for s in range(3):
+                endo[nxt, s, span, :] += (
+                    gain[:, s * points:(s + 1) * points] + block_e[s, pl.ds(i * width, width), :]
+                )
+
+    def finish_inside(nxt):
+        span = pl.ds(width, rows - 2 * width)
+        gain = dot(put_e[span, :], endo_flux())
+        for s in range(3):
+            endo[nxt, s, span, :] += gain[:, s * points:(s + 1) * points]
 
     def finish_musc(nxt):
         flux = jnp.concatenate([block_m[s, pl.ds(2 * length, 2 * n), :] for s in range(3)], axis=1)
@@ -339,6 +404,7 @@
             musc[nxt, s, first, :] = musc[nxt, s, first, :] + block_m[s, pl.ds(0, length), :]
             musc[nxt, s, final, :] = musc[nxt, s, final, :] + block_m[s, pl.ds(length, length), :]
 
+    start_far(0)
     pack(0)
     launch(0)
     start_ends(0)
@@ -349,14 +415,18 @@
         nxt = 1 - par
         local_part(par, nxt, False)
         collect(par)
-        from_outside(par, False)
+        endo_outside(par)
+        finish_ends(nxt)
+        start_far(nxt)
+        musc_outside(par)
+        pick()
         pl.when(t > 0)(lambda: messages(nxt).wait_send())
         pack(nxt)
         launch(nxt)
-        finish_endo(nxt)
         start_ends(nxt)
         finish_musc(nxt)
         start_sides(nxt)
+        finish_inside(nxt)
         return carry
 
     lax.fori_loop(0, TIME_STEPS - 1, step, 0)
@@ -364,10 +434,12 @@
     nxt = 1 - par
     local_part(par, nxt, True)
     collect(par)
-    from_outside(par, True)
-    finish_endo(nxt)
+    endo_outside(par)
+    finish_ends(nxt)
+    finish_inside(nxt)
     store_e = pltpu.make_async_copy(endo.at[nxt], endo_out, in_sems.at[0])
     store_e.start()
+    musc_outside(par)
     finish_musc(nxt)
     store_m = pltpu.make_async_copy(musc.at[nxt], musc_out, in_sems.at[1])
     store_m.start()
@@ -375,6 +447,17 @@
     messages(par).wait_send()
     store_e.wait()
     store_m.wait()
+
+
+def hand_over(endo_from, musc_from, endo_to, musc_to, sems):
+    copies = []
+    for layer, (a, b) in enumerate(((endo_from, endo_to), (musc_from, musc_to))):
+        for s in range(a.shape[0]):
+            copies.append(pltpu.make_async_copy(a.at[s], b.at[s], sems.at[layer, s]))
+    for copy in copies:
+        copy.start()
+    for copy in copies:
+        copy.wait()
 
 
 def local(
@@ -434,6 +517,8 @@
             dma((6,)), dma, dma((2,)), dma((2,)),
             dma((2,)), dma((2, 2)), dma((2,)), dma((2, 2)),
             dma((2,)),
+            pltpu.VMEM((2, 2, species, width - width // 2, points), F32),
+            dma((2, 2)), dma((2,)),
         ],
         compiler_params=pltpu.CompilerParams(
             collective_id=0, has_side_effects=True, vmem_limit_bytes=60 * 1024 * 1024
@@ -446,6 +531,18 @@
         meta[:, None, :],
         endo_inverse, muscle_inverse,
     )
+    endo_next, musc_next = pl.pallas_call(
+        hand_over,
+        out_shape=(
+            jax.ShapeDtypeStruct((species, rows, points), F32),
+            jax.ShapeDtypeStruct((species, musc_rows, points), F32),
+        ),
+        in_specs=[anywhere] * 2,
+        out_specs=(anywhere, anywhere),
+        scratch_shapes=[dma((2, species))],
+        compiler_params=pltpu.CompilerParams(vmem_limit_bytes=60 * 1024 * 1024),
+        name="hand_over",
+    )(endo_next, musc_next)
     return endo_next.reshape(endothelium.shape), musc_next.reshape(muscle.shape)
 
 

time: 86.8 us -> 130 us (1.50)
  Pallas kernels: 80.6 us -> 127 us
  local copies, waits for them, and re-layouts: 4.36 us -> 1.34 us
    pallas_call x0 -> x1, Pallas kernels: none -> 48.8 us  [local(): pl.pallas_call(hand_over, out_shape=(jax.ShapeDtypeStruct((species, rows,...]
    unnamed x10 -> x6, local copies, waits for them, and re-layouts: 4.36 us -> 1.34 us
    pallas_call x1, Pallas kernels: 80.6 us -> 78 us  [local(): pl.pallas_call(body, out_shape=(jax.ShapeDtypeStruct((species, rows, poin...]
where the time goes in v2:
time: 130 us
  Pallas kernels  127 us (98%)
  local copies, waits for them, and re-layouts  1.34 us (1%)
    pallas_call x1, Pallas kernels, local(): pl.pallas_call(body, out_shape=(jax.ShapeDtypeStruct((species, rows, poin...  78 us
    pallas_call x1, Pallas kernels, local(): pl.pallas_call(hand_over, out_shape=(jax.ShapeDtypeStruct((species, rows,...  48.8 us

profile of v2, /device:TPU:1, one launch (start us, length us, event | category | flops | bytes accessed | tf_op | source)
XLA Modules:
  0.0 129.7 jit_solution(9939671823412264400)
XLA Ops:
  0.7 0.0 copy-start.1
  0.7 0.0 copy-start
  0.7 0.7 copy-done.1
  1.3 0.0 copy-done
  1.4 0.0 copy-start.2
  1.4 0.7 copy-done.2
  2.0 0.8 compare_select_fusion.meta_in
  2.9 78.0 %cable_steps.1 = (f32[3,512,128]{2,1,0:T(8,128)}, f32[3,512,128]{2,1,0:T(8,128)}) custom-call(f32[3,512,128]{2,1,0:T(8,128)} %bitcast.16, f32[3,512,128]{2,1,0:T(8,128)} %bitcast.17, f32[512,128]{1,0:T(8,128)} %bitcast.18, s32[32,1,128]{2,1,0:T(1,128)} %compare_select_fusion.meta_in, f32[3,128,128]{2,1,0:T(8,128)} %endo_inv_in.1, f32[3,128,128]{2,1,0:T(8,128)} %musc_inv_in.1), custom_call_target="tpu_custom_call" | custom-call | tf_op jit(solution)/shard_map/cable_steps/pallas_call | solution.py:482
  80.9 48.8 %hand_over.1 = (f32[3,512,128]{2,1,0:T(8,128)}, f32[3,512,128]{2,1,0:T(8,128)}) custom-call(f32[3,512,128]{2,1,0:T(8,128)} %get-tuple-element.6.endo_from, f32[3,512,128]{2,1,0:T(8,128)} %get-tuple-element.7.musc_from), custom_call_target="tpu_custom_call" | custom-call | tf_op jit(solution)/shard_map/hand_over/pallas_call | solution.py:534
  (4 shorter events, 0.0 us)
Async XLA Ops:
  0.7 0.7 copy-start.1
  0.7 0.7 copy-start
  1.4 0.7 copy-start.2

commit v3 on v2

--- a/solution.py
+++ b/solution.py
@@ -47,7 +47,7 @@
     endo_in, musc_in, agonist_in, meta_in, endo_inv_in, musc_inv_in,
     endo_out, musc_out,
     endo, musc, halo_low, halo_high, edge_out, edge_left, edge_right,
-    send, recv, picked, base_rows, weights, take_e, take_m, put_e, put_m, mix_e, mix_m, rhs,
+    send, recv, picked, base_rows, weights, take_e, take_m, put_e, put_m, mix_e, mix_m, same_e, same_m, rhs,
     block_e, block_m, agonist, meta, meta_recv, endo_inv, musc_inv,
     in_sems, own_sem, send_sem, recv_sem, halo_send, halo_recv, edge_send, edge_recv,
     meta_sems, relay, relay_recv, relay_send,
@@ -67,8 +67,8 @@
     turn = lax.rem(ax, 4)
     up_far = (turn == 3) & (ax < n_ax - 1)
     down_far = (turn == 0) & (ax > 0)
-    relay_up = (turn == 3) & (ax > 3)
-    relay_down = (turn == 0) & (ax < n_ax - 4)
+    relay_up = (turn == 0) & (ax < n_ax - 4)
+    relay_down = (turn == 3) & (ax > 3)
     turned = [lax.rem(circ + c, n_circ) for c in range(n_circ)]
 
     def each_peer(act):
@@ -141,9 +141,8 @@
     sent = meta[:, 0, :]
     ids = jnp.concatenate([sent[:, 2:3], sent[:, 3:4]], axis=0)
     chosen, same = choose(ids, take_e, put_e)
-    mix_e[...] = jnp.concatenate(
-        [chosen[:, :width], chosen[:, rows - width:], same], axis=1
-    ).astype(BF16)
+    mix_e[...] = jnp.concatenate([chosen[:, :width], chosen[:, rows - width:]], axis=1).astype(BF16)
+    same_e[...] = same.astype(BF16)
 
     def gather(layer, s, values, out):
         take = take_e if layer == 0 else take_m
@@ -170,10 +169,10 @@
         [
             jnp.where(starts == ids, 1.0, 0.0),
             jnp.where(starts + (cycle - 1) == ids, 1.0, 0.0),
-            same,
         ],
         axis=1,
     ).astype(BF16)
+    same_m[...] = same.astype(BF16)
     for s in range(3):
         gather(1, s, musc[0, s], picked)
     told.wait_send()
@@ -227,7 +226,7 @@
         return pltpu.make_async_remote_copy(
             src_ref=cells(par, up, half, width - half), dst_ref=relay.at[par, int(up)],
             send_sem=halo_send.at[int(up)], recv_sem=relay_recv.at[par, int(up)],
-            device_id=(ax + 4 if up else ax - 4, circ), device_id_type=MESH,
+            device_id=(ax - 3 if up else ax + 3, circ), device_id_type=MESH,
         )
 
     def from_relay(par, up):
@@ -235,7 +234,7 @@
         return pltpu.make_async_remote_copy(
             src_ref=relay.at[par, int(up)], dst_ref=dst.at[par, :, pl.ds(half, width - half)],
             send_sem=relay_send.at[int(up)], recv_sem=halo_recv.at[par, int(up)],
-            device_id=(ax - 3 if up else ax + 3, circ), device_id_type=MESH,
+            device_id=(ax + 4 if up else ax - 4, circ), device_id_type=MESH,
         )
 
     def start_far(par):
@@ -328,9 +327,11 @@
                 if not last:
                     gather(layer, s, value, base_rows)
 
-    def collect(par):
+    def collect_messages(par):
         own_copy(par).wait()
         messages(par).wait_recv()
+
+    def collect_halos(par):
         for copy in sides(par):
             copy.wait()
         passed_on(par)
@@ -352,41 +353,56 @@
             [flat[pl.ds(k + slot, n, stride=16), :] for slot in range(2)], axis=0
         )
 
-    def endo_outside(par):
+    def inverted(layer, s, value):
+        return folded(dot(side_by_side(value), weights[layer * 3 + s]))
+
+    def take_messages(par, last=False):
         for s in range(3):
             flux = (DT * COUPLING[s]) * (arrived(par, 1, s) - picked[s])
+            flux = inverted(0, s, flux)
+            block_e[s, pl.ds(2 * width, 2 * n), :] = flux
+            if not last:
+                picked[s] = base_rows[s] + folded(dot(same_e[...], side_by_side(flux)))
+            flux = (DT * COUPLING[s]) * (arrived(par, 0, s) - picked[3 + s])
+            flux = inverted(1, s, flux)
+            block_m[s, pl.ds(2 * length, 2 * n), :] = flux
+            if not last:
+                picked[3 + s] = base_rows[3 + s] + folded(dot(same_m[...], side_by_side(flux)))
+
+    def take_halos(par, last=False):
+        for s in range(3):
             gap = DT * ENDO_GAP[s]
-            value = jnp.concatenate([gap * halo_low[par, s], gap * halo_high[par, s], flux], axis=0)
-            block_e[s] = folded(dot(side_by_side(value), weights[s]))
-
-    def musc_outside(par):
-        for s in range(3):
-            flux = (DT * COUPLING[s]) * (arrived(par, 0, s) - picked[3 + s])
+            value = jnp.concatenate([gap * halo_low[par, s], gap * halo_high[par, s]], axis=0)
+            value = inverted(0, s, value)
+            block_e[s, pl.ds(0, 2 * width), :] = value
+            if not last:
+                picked[s] += folded(dot(mix_e[...], side_by_side(value)))
             gap = DT * MUSC_GAP[s]
             span = pl.ds(s * length, length)
             value = jnp.concatenate(
-                [gap * edge_left[par, span, :], gap * edge_right[par, span, :], flux], axis=0
+                [gap * edge_left[par, span, :], gap * edge_right[par, span, :]], axis=0
             )
-            block_m[s] = folded(dot(side_by_side(value), weights[3 + s]))
-
-    def pick():
-        for s in range(3):
-            picked[s] = base_rows[s] + folded(dot(mix_e[...], side_by_side(block_e[s])))
-            picked[3 + s] = base_rows[3 + s] + folded(dot(mix_m[...], side_by_side(block_m[s])))
+            value = inverted(1, s, value)
+            block_m[s, pl.ds(0, 2 * length), :] = value
+            if not last:
+                picked[3 + s] += folded(dot(mix_m[...], side_by_side(value)))
 
     def endo_flux():
         flux = jnp.concatenate([block_e[s, pl.ds(2 * width, 2 * n), :] for s in range(3)], axis=1)
         return jnp.concatenate(halves(flux), axis=0)
 
-    def finish_ends(nxt):
+    def flux_at_ends(nxt):
         flux = endo_flux()
-        for i, first in enumerate((0, rows - width)):
+        for first in (0, rows - width):
             span = pl.ds(first, width)
             gain = dot(put_e[span, :], flux)
             for s in range(3):
-                endo[nxt, s, span, :] += (
-                    gain[:, s * points:(s + 1) * points] + block_e[s, pl.ds(i * width, width), :]
-                )
+                endo[nxt, s, span, :] += gain[:, s * points:(s + 1) * points]
+
+    def halo_at_ends(nxt):
+        for s in range(3):
+            endo[nxt, s, pl.ds(0, width), :] += block_e[s, pl.ds(0, width), :]
+            endo[nxt, s, pl.ds(rows - width, width), :] += block_e[s, pl.ds(width, width), :]
 
     def finish_inside(nxt):
         span = pl.ds(width, rows - 2 * width)
@@ -414,12 +430,13 @@
         par = lax.rem(t, 2)
         nxt = 1 - par
         local_part(par, nxt, False)
-        collect(par)
-        endo_outside(par)
-        finish_ends(nxt)
+        collect_messages(par)
+        take_messages(par)
+        flux_at_ends(nxt)
+        collect_halos(par)
+        take_halos(par)
+        halo_at_ends(nxt)
         start_far(nxt)
-        musc_outside(par)
-        pick()
         pl.when(t > 0)(lambda: messages(nxt).wait_send())
         pack(nxt)
         launch(nxt)
@@ -433,13 +450,15 @@
     par = (TIME_STEPS - 1) % 2
     nxt = 1 - par
     local_part(par, nxt, True)
-    collect(par)
-    endo_outside(par)
-    finish_ends(nxt)
+    collect_messages(par)
+    take_messages(par, True)
+    flux_at_ends(nxt)
     finish_inside(nxt)
+    collect_halos(par)
+    take_halos(par, True)
+    halo_at_ends(nxt)
     store_e = pltpu.make_async_copy(endo.at[nxt], endo_out, in_sems.at[0])
     store_e.start()
-    musc_outside(par)
     finish_musc(nxt)
     store_m = pltpu.make_async_copy(musc.at[nxt], musc_out, in_sems.at[1])
     store_m.start()
@@ -449,15 +468,21 @@
     store_m.wait()
 
 
-def hand_over(endo_from, musc_from, endo_to, musc_to, sems):
-    copies = []
-    for layer, (a, b) in enumerate(((endo_from, endo_to), (musc_from, musc_to))):
-        for s in range(a.shape[0]):
-            copies.append(pltpu.make_async_copy(a.at[s], b.at[s], sems.at[layer, s]))
-    for copy in copies:
-        copy.start()
-    for copy in copies:
-        copy.wait()
+def hand_over(endo_from, musc_from, endo_to, musc_to, endo, musc, sems, out_sems):
+    pairs = []
+    for layer, (a, held, b) in enumerate(((endo_from, endo, endo_to), (musc_from, musc, musc_to))):
+        for s in range(held.shape[0]):
+            pairs.append((
+                pltpu.make_async_copy(a.at[s], held.at[s], sems.at[layer, s]),
+                pltpu.make_async_copy(held.at[s], b.at[s], out_sems.at[layer, s]),
+            ))
+    for load, store in pairs:
+        load.start()
+    for load, store in pairs:
+        load.wait()
+        store.start()
+    for load, store in pairs:
+        store.wait()
 
 
 def local(
@@ -504,8 +529,10 @@
             pltpu.VMEM((slots * n, musc_rows), BF16),
             pltpu.VMEM((rows, 2 * slots * n), BF16),
             pltpu.VMEM((musc_rows, 2 * slots * n), BF16),
-            pltpu.VMEM((slots * n, 2 * width + slots * n), BF16),
-            pltpu.VMEM((slots * n, 2 * length + slots * n), BF16),
+            pltpu.VMEM((slots * n, 2 * width), BF16),
+            pltpu.VMEM((slots * n, 2 * length), BF16),
+            pltpu.VMEM((slots * n, slots * n), BF16),
+            pltpu.VMEM((slots * n, slots * n), BF16),
             pltpu.VMEM((6, max(rows, musc_rows), 2 * points), BF16),
             pltpu.VMEM((species, 2 * width + slots * n, points), F32),
             pltpu.VMEM((species, 2 * length + slots * n, points), F32),
@@ -539,7 +566,11 @@
         ),
         in_specs=[anywhere] * 2,
         out_specs=(anywhere, anywhere),
-        scratch_shapes=[dma((2, species))],
+        scratch_shapes=[
+            pltpu.VMEM((species, rows, points), F32),
+            pltpu.VMEM((species, musc_rows, points), F32),
+            dma((2, species)), dma((2, species)),
+        ],
         compiler_params=pltpu.CompilerParams(vmem_limit_bytes=60 * 1024 * 1024),
         name="hand_over",
     )(endo_next, musc_next)

time: 130 us -> 92.6 us (0.71)
  Pallas kernels: 127 us -> 89.4 us
    pallas_call x1, Pallas kernels: 48.8 us -> 2.19 us  [local(): pl.pallas_call(hand_over, out_shape=(jax.ShapeDtypeStruct((species, rows,...]
    pallas_call x1, Pallas kernels: 78 us -> 87.2 us  [local(): pl.pallas_call(body, out_shape=(jax.ShapeDtypeStruct((species, rows, poin...]
where the time goes in v3:
time: 92.6 us; the launch traced here: 92.3 us
  Pallas kernels  89.4 us (97%)
  local copies, waits for them, and re-layouts  1.34 us (1%)
    pallas_call x1, Pallas kernels, local(): pl.pallas_call(body, out_shape=(jax.ShapeDtypeStruct((species, rows, poin...  87.2 us
    pallas_call x1, Pallas kernels, local(): pl.pallas_call(hand_over, out_shape=(jax.ShapeDtypeStruct((species, rows,...  2.19 us

profile of v3, /device:TPU:1, one launch (start us, length us, event | category | flops | bytes accessed | tf_op | source)
XLA Modules:
  0.0 92.3 jit_solution(6217727229672226103)
XLA Ops:
  0.7 0.0 copy-start.1
  0.7 0.0 copy-start
  0.7 0.7 copy-done.1
  1.3 0.0 copy-done
  1.4 0.0 copy-start.2
  1.4 0.7 copy-done.2
  2.0 0.8 compare_select_fusion.meta_in
  2.9 87.2 %cable_steps.1 = (f32[3,512,128]{2,1,0:T(8,128)}, f32[3,512,128]{2,1,0:T(8,128)}) custom-call(f32[3,512,128]{2,1,0:T(8,128)} %bitcast.16, f32[3,512,128]{2,1,0:T(8,128)} %bitcast.17, f32[512,128]{1,0:T(8,128)} %bitcast.18, s32[32,1,128]{2,1,0:T(1,128)} %compare_select_fusion.meta_in, f32[3,128,128]{2,1,0:T(8,128)} %endo_inv_in.1, f32[3,128,128]{2,1,0:T(8,128)} %musc_inv_in.1), custom_call_target="tpu_custom_call" | custom-call | tf_op jit(solution)/shard_map/cable_steps/pallas_call | solution.py:507
  90.1 2.2 %hand_over.1 = (f32[3,512,128]{2,1,0:T(8,128)}, f32[3,512,128]{2,1,0:T(8,128)}) custom-call(f32[3,512,128]{2,1,0:T(8,128)} %get-tuple-element.6.endo_from, f32[3,512,128]{2,1,0:T(8,128)} %get-tuple-element.7.musc_from), custom_call_target="tpu_custom_call" | custom-call | tf_op jit(solution)/shard_map/hand_over/pallas_call | solution.py:561
  (4 shorter events, 0.0 us)
Async XLA Ops:
  0.7 0.7 copy-start.1
  0.7 0.7 copy-start
  1.4 0.7 copy-start.2

commit v4 on v3

--- a/solution.py
+++ b/solution.py
@@ -44,11 +44,11 @@
 
 def kernel(
     sizes,
-    endo_in, musc_in, agonist_in, meta_in, endo_inv_in, musc_inv_in,
+    endo_in, musc_in, agonist_in, target_in, cell_in, count_in, endo_inv_in, musc_inv_in,
     endo_out, musc_out,
     endo, musc, halo_low, halo_high, edge_out, edge_left, edge_right,
     send, recv, picked, base_rows, weights, take_e, take_m, put_e, put_m, mix_e, mix_m, same_e, same_m, rhs,
-    block_e, block_m, agonist, meta, meta_recv, endo_inv, musc_inv,
+    block_e, block_m, agonist, meta, meta_recv, endo_inv, musc_inv, targets, starts_at, counts,
     in_sems, own_sem, send_sem, recv_sem, halo_send, halo_recv, edge_send, edge_recv,
     meta_sems, relay, relay_recv, relay_send,
 ):
@@ -67,8 +67,8 @@
     turn = lax.rem(ax, 4)
     up_far = (turn == 3) & (ax < n_ax - 1)
     down_far = (turn == 0) & (ax > 0)
-    relay_up = (turn == 0) & (ax < n_ax - 4)
-    relay_down = (turn == 3) & (ax > 3)
+    relay_up = (turn == 3) & (ax > 3)
+    relay_down = (turn == 0) & (ax < n_ax - 4)
     turned = [lax.rem(circ + c, n_circ) for c in range(n_circ)]
 
     def each_peer(act):
@@ -86,8 +86,9 @@
         pltpu.make_async_copy(a, b, in_sems.at[i])
         for i, (a, b) in enumerate(
             (
-                (meta_in, meta), (endo_in, endo.at[0]), (musc_in, musc.at[0]),
+                (target_in, targets), (endo_in, endo.at[0]), (musc_in, musc.at[0]),
                 (endo_inv_in, endo_inv), (musc_inv_in, musc_inv), (agonist_in, agonist),
+                (cell_in, starts_at), (count_in, counts),
             )
         )
     ]
@@ -109,8 +110,67 @@
     def _():
         halo_high[...] = jnp.zeros_like(halo_high)
 
-    loads[0].wait()
+    for i in (0, 6, 7):
+        loads[i].wait()
+    live = lax.broadcasted_iota(jnp.int32, targets.shape, 0) < counts[...]
+    nowhere = rows + musc_rows
+    table = jnp.concatenate(
+        [
+            jnp.where(live, targets[...], nowhere).astype(F32),
+            jnp.where(live, starts_at[...], nowhere).astype(F32),
+            jnp.zeros((4, n), F32),
+        ],
+        axis=0,
+    )
+    if n % 128:
+        table = jnp.concatenate([table, jnp.zeros((8, 128 - n % 128), F32)], axis=1)
+    columns = table.T[:n]
+    meta[:, 0, :] = jnp.concatenate(
+        [columns, jnp.zeros((n, points - 8), F32)], axis=1
+    ).astype(jnp.int32)
     pl.semaphore_wait(barrier, n - 1)
+
+    def cells(par, from_top, start, count):
+        first = rows - width if from_top else 0
+        return endo.at[par, :, pl.ds(first + start, count)]
+
+    def end_copy(par, up, start, count):
+        dst = halo_low if up else halo_high
+        return pltpu.make_async_remote_copy(
+            src_ref=cells(par, up, start, count), dst_ref=dst.at[par, :, pl.ds(start, count)],
+            send_sem=halo_send.at[int(up)], recv_sem=halo_recv.at[par, int(up)],
+            device_id=(ax + 1 if up else ax - 1, circ), device_id_type=MESH,
+        )
+
+    def to_relay(par, up):
+        return pltpu.make_async_remote_copy(
+            src_ref=cells(par, up, half, width - half), dst_ref=relay.at[par, int(up)],
+            send_sem=halo_send.at[int(up)], recv_sem=relay_recv.at[par, int(up)],
+            device_id=(ax + 4 if up else ax - 4, circ), device_id_type=MESH,
+        )
+
+    def from_relay(par, up):
+        dst = halo_low if up else halo_high
+        return pltpu.make_async_remote_copy(
+            src_ref=relay.at[par, int(up)], dst_ref=dst.at[par, :, pl.ds(half, width - half)],
+            send_sem=relay_send.at[int(up)], recv_sem=halo_recv.at[par, int(up)],
+            device_id=(ax - 3 if up else ax + 3, circ), device_id_type=MESH,
+        )
+
+    def start_far(par):
+        if corners:
+            pl.when(up_far)(to_relay(par, True).start)
+            pl.when(down_far)(to_relay(par, False).start)
+
+    def start_ends(par):
+        if corners:
+            pl.when(up_far)(end_copy(par, True, 0, half).start)
+            pl.when(down_far)(end_copy(par, False, 0, half).start)
+            pl.when((ax < n_ax - 1) & (turn != 3))(end_copy(par, True, 0, width).start)
+            pl.when((ax > 0) & (turn != 0))(end_copy(par, False, 0, width).start)
+        else:
+            pl.when(ax < n_ax - 1)(end_copy(par, True, 0, width).start)
+            pl.when(ax > 0)(end_copy(par, False, 0, width).start)
 
     def tell(pa, pc):
         pltpu.make_async_remote_copy(
@@ -120,6 +180,9 @@
         ).start()
 
     each_peer(tell)
+    loads[1].wait()
+    start_far(0)
+    start_ends(0)
     own_meta = pltpu.make_async_copy(meta.at[me], meta_recv.at[me], own_sem)
     own_meta.start()
 
@@ -148,7 +211,6 @@
         take = take_e if layer == 0 else take_m
         out[layer * 3 + s] = folded(dot(take[...], side_by_side(values)))
 
-    loads[1].wait()
     loads[2].wait()
     loads[5].wait()
     for s in range(3):
@@ -210,48 +272,6 @@
         each_peer(post)
         own_copy(par).start()
 
-    def cells(par, from_top, start, count):
-        first = rows - width if from_top else 0
-        return endo.at[par, :, pl.ds(first + start, count)]
-
-    def end_copy(par, up, start, count):
-        dst = halo_low if up else halo_high
-        return pltpu.make_async_remote_copy(
-            src_ref=cells(par, up, start, count), dst_ref=dst.at[par, :, pl.ds(start, count)],
-            send_sem=halo_send.at[int(up)], recv_sem=halo_recv.at[par, int(up)],
-            device_id=(ax + 1 if up else ax - 1, circ), device_id_type=MESH,
-        )
-
-    def to_relay(par, up):
-        return pltpu.make_async_remote_copy(
-            src_ref=cells(par, up, half, width - half), dst_ref=relay.at[par, int(up)],
-            send_sem=halo_send.at[int(up)], recv_sem=relay_recv.at[par, int(up)],
-            device_id=(ax - 3 if up else ax + 3, circ), device_id_type=MESH,
-        )
-
-    def from_relay(par, up):
-        dst = halo_low if up else halo_high
-        return pltpu.make_async_remote_copy(
-            src_ref=relay.at[par, int(up)], dst_ref=dst.at[par, :, pl.ds(half, width - half)],
-            send_sem=relay_send.at[int(up)], recv_sem=halo_recv.at[par, int(up)],
-            device_id=(ax + 4 if up else ax - 4, circ), device_id_type=MESH,
-        )
-
-    def start_far(par):
-        if corners:
-            pl.when(up_far)(to_relay(par, True).start)
-            pl.when(down_far)(to_relay(par, False).start)
-
-    def start_ends(par):
-        if corners:
-            pl.when(up_far)(end_copy(par, True, 0, half).start)
-            pl.when(down_far)(end_copy(par, False, 0, half).start)
-            pl.when((ax < n_ax - 1) & (turn != 3))(end_copy(par, True, 0, width).start)
-            pl.when((ax > 0) & (turn != 0))(end_copy(par, False, 0, width).start)
-        else:
-            pl.when(ax < n_ax - 1)(end_copy(par, True, 0, width).start)
-            pl.when(ax > 0)(end_copy(par, False, 0, width).start)
-
     def pass_on(par):
         if not corners:
             return
@@ -304,6 +324,8 @@
                     value = u[s] + DT * (parts[s] + ENDO_GAP[s] * lap)
                     rhs[s, here, :] = side_by_side(value)
 
+        pass_on(par)
+
         def musc_base(a, carry):
             here = pl.ds(pl.multiple_of(a * cycle, cycle), cycle)
             place_in = lax.broadcasted_iota(jnp.int32, (cycle, points), 0)
@@ -318,7 +340,6 @@
             return carry
 
         lax.fori_loop(0, length, musc_base, 0)
-        pass_on(par)
 
         for layer, state in ((0, endo), (1, musc)):
             for s in range(3):
@@ -420,11 +441,9 @@
             musc[nxt, s, first, :] = musc[nxt, s, first, :] + block_m[s, pl.ds(0, length), :]
             musc[nxt, s, final, :] = musc[nxt, s, final, :] + block_m[s, pl.ds(length, length), :]
 
-    start_far(0)
+    start_sides(0)
     pack(0)
     launch(0)
-    start_ends(0)
-    start_sides(0)
 
     def step(t, carry):
         par = lax.rem(t, 2)
@@ -437,10 +456,10 @@
         take_halos(par)
         halo_at_ends(nxt)
         start_far(nxt)
+        start_ends(nxt)
         pl.when(t > 0)(lambda: messages(nxt).wait_send())
         pack(nxt)
         launch(nxt)
-        start_ends(nxt)
         finish_musc(nxt)
         start_sides(nxt)
         finish_inside(nxt)
@@ -495,12 +514,6 @@
     rows = endo_ax * width
     musc_rows = length * cycle
     slots = proj_cell.shape[2]
-    lane = jnp.arange(points, dtype=jnp.int32)[None, :]
-    target, cell = proj_target[0], proj_cell[0]
-    live = lane % slots < proj_count[0][:, None]
-    first = jnp.where(lane == 0, target[:, 0:1], target[:, 1:2])
-    second = jnp.where(lane == slots, cell[:, 0:1], cell[:, 1:2])
-    meta = jnp.where(live, jnp.where(lane < slots, first, second), rows + musc_rows)
     anywhere = pl.BlockSpec(memory_space=pl.ANY)
     dma = pltpu.SemaphoreType.DMA
     body = functools.partial(kernel, (n_ax, n_circ, width, length, cycle))
@@ -510,7 +523,7 @@
             jax.ShapeDtypeStruct((species, rows, points), F32),
             jax.ShapeDtypeStruct((species, musc_rows, points), F32),
         ),
-        in_specs=[anywhere] * 6,
+        in_specs=[anywhere] * 8,
         out_specs=(anywhere, anywhere),
         scratch_shapes=[
             pltpu.VMEM((2, species, rows, points), F32),
@@ -541,7 +554,10 @@
             pltpu.VMEM((n, 1, points), jnp.int32),
             pltpu.VMEM((species, points, points), F32),
             pltpu.VMEM((species, points, points), F32),
-            dma((6,)), dma, dma((2,)), dma((2,)),
+            pltpu.VMEM((slots, n), jnp.int32),
+            pltpu.VMEM((slots, n), jnp.int32),
+            pltpu.VMEM((1, n), jnp.int32),
+            dma((8,)), dma, dma((2,)), dma((2,)),
             dma((2,)), dma((2, 2)), dma((2,)), dma((2, 2)),
             dma((2,)),
             pltpu.VMEM((2, 2, species, width - width // 2, points), F32),
@@ -555,7 +571,7 @@
         endothelium.reshape(species, rows, points),
         muscle.reshape(species, musc_rows, points),
         agonist.reshape(rows, points),
-        meta[:, None, :],
+        proj_target[0].T, proj_cell[0].T, proj_count,
         endo_inverse, muscle_inverse,
     )
     endo_next, musc_next = pl.pallas_call(

time: 92.6 us -> 91.3 us (0.986)
  local copies, waits for them, and re-layouts: 1.34 us -> 0 us
    unnamed x6 -> x0, local copies, waits for them, and re-layouts: 1.34 us -> none
where the time goes in v4:
time: 91.3 us; the launch traced here: 90.8 us
  Pallas kernels  90.1 us (99%)
    pallas_call x1, Pallas kernels, local(): pl.pallas_call(body, out_shape=(jax.ShapeDtypeStruct((species, rows, poin...  88 us
    pallas_call x1, Pallas kernels, local(): pl.pallas_call(hand_over, out_shape=(jax.ShapeDtypeStruct((species, rows,...  2.19 us

profile of v4, /device:TPU:1, one launch (start us, length us, event | category | flops | bytes accessed | tf_op | source)
XLA Modules:
  0.0 90.8 jit_solution(2379362997513128965)
XLA Ops:
  0.6 88.0 %cable_steps.1 = (f32[3,512,128]{2,1,0:T(8,128)}, f32[3,512,128]{2,1,0:T(8,128)}) custom-call(f32[3,512,128]{2,1,0:T(8,128)} %bitcast.11, f32[3,512,128]{2,1,0:T(8,128)} %bitcast.12, f32[512,128]{1,0:T(8,128)} %bitcast.13, s32[2,32]{1,0:T(2,128)} %bitcast.14, s32[2,32]{1,0:T(2,128)} %bitcast.15, s32[1,32]{1,0:T(1,128)} %count_in.1, ...), custom_call_target="tpu_custom_call" | custom-call | tf_op jit(solution)/shard_map/cable_steps/pallas_call | solution.py:520
  88.6 2.2 %hand_over.1 = (f32[3,512,128]{2,1,0:T(8,128)}, f32[3,512,128]{2,1,0:T(8,128)}) custom-call(f32[3,512,128]{2,1,0:T(8,128)} %get-tuple-element.6.endo_from, f32[3,512,128]{2,1,0:T(8,128)} %get-tuple-element.7.musc_from), custom_call_target="tpu_custom_call" | custom-call | tf_op jit(solution)/shard_map/hand_over/pallas_call | solution.py:577

commit v5 on v2

--- a/solution.py
+++ b/solution.py
@@ -44,11 +44,11 @@
 
 def kernel(
     sizes,
-    endo_in, musc_in, agonist_in, meta_in, endo_inv_in, musc_inv_in,
+    endo_in, musc_in, agonist_in, target_in, cell_in, count_in, endo_inv_in, musc_inv_in,
     endo_out, musc_out,
     endo, musc, halo_low, halo_high, edge_out, edge_left, edge_right,
     send, recv, picked, base_rows, weights, take_e, take_m, put_e, put_m, mix_e, mix_m, rhs,
-    block_e, block_m, agonist, meta, meta_recv, endo_inv, musc_inv,
+    block_e, block_m, agonist, meta, meta_recv, endo_inv, musc_inv, targets, starts_at, counts,
     in_sems, own_sem, send_sem, recv_sem, halo_send, halo_recv, edge_send, edge_recv,
     meta_sems, relay, relay_recv, relay_send,
 ):
@@ -86,8 +86,9 @@
         pltpu.make_async_copy(a, b, in_sems.at[i])
         for i, (a, b) in enumerate(
             (
-                (meta_in, meta), (endo_in, endo.at[0]), (musc_in, musc.at[0]),
+                (target_in, targets), (endo_in, endo.at[0]), (musc_in, musc.at[0]),
                 (endo_inv_in, endo_inv), (musc_inv_in, musc_inv), (agonist_in, agonist),
+                (cell_in, starts_at), (count_in, counts),
             )
         )
     ]
@@ -109,7 +110,24 @@
     def _():
         halo_high[...] = jnp.zeros_like(halo_high)
 
-    loads[0].wait()
+    for i in (0, 6, 7):
+        loads[i].wait()
+    live = lax.broadcasted_iota(jnp.int32, targets.shape, 0) < counts[...]
+    nowhere = rows + musc_rows
+    table = jnp.concatenate(
+        [
+            jnp.where(live, targets[...], nowhere).astype(F32),
+            jnp.where(live, starts_at[...], nowhere).astype(F32),
+            jnp.zeros((4, n), F32),
+        ],
+        axis=0,
+    )
+    if n % 128:
+        table = jnp.concatenate([table, jnp.zeros((8, 128 - n % 128), F32)], axis=1)
+    columns = table.T[:n]
+    meta[:, 0, :] = jnp.concatenate(
+        [columns, jnp.zeros((n, points - 8), F32)], axis=1
+    ).astype(jnp.int32)
     pl.semaphore_wait(barrier, n - 1)
 
     def tell(pa, pc):
@@ -449,15 +467,21 @@
     store_m.wait()
 
 
-def hand_over(endo_from, musc_from, endo_to, musc_to, sems):
-    copies = []
-    for layer, (a, b) in enumerate(((endo_from, endo_to), (musc_from, musc_to))):
-        for s in range(a.shape[0]):
-            copies.append(pltpu.make_async_copy(a.at[s], b.at[s], sems.at[layer, s]))
-    for copy in copies:
-        copy.start()
-    for copy in copies:
-        copy.wait()
+def hand_over(endo_from, musc_from, endo_to, musc_to, endo, musc, sems, out_sems):
+    pairs = []
+    for layer, (a, held, b) in enumerate(((endo_from, endo, endo_to), (musc_from, musc, musc_to))):
+        for s in range(held.shape[0]):
+            pairs.append((
+                pltpu.make_async_copy(a.at[s], held.at[s], sems.at[layer, s]),
+                pltpu.make_async_copy(held.at[s], b.at[s], out_sems.at[layer, s]),
+            ))
+    for load, store in pairs:
+        load.start()
+    for load, store in pairs:
+        load.wait()
+        store.start()
+    for load, store in pairs:
+        store.wait()
 
 
 def local(
@@ -470,12 +494,6 @@
     rows = endo_ax * width
     musc_rows = length * cycle
     slots = proj_cell.shape[2]
-    lane = jnp.arange(points, dtype=jnp.int32)[None, :]
-    target, cell = proj_target[0], proj_cell[0]
-    live = lane % slots < proj_count[0][:, None]
-    first = jnp.where(lane == 0, target[:, 0:1], target[:, 1:2])
-    second = jnp.where(lane == slots, cell[:, 0:1], cell[:, 1:2])
-    meta = jnp.where(live, jnp.where(lane < slots, first, second), rows + musc_rows)
     anywhere = pl.BlockSpec(memory_space=pl.ANY)
     dma = pltpu.SemaphoreType.DMA
     body = functools.partial(kernel, (n_ax, n_circ, width, length, cycle))
@@ -485,7 +503,7 @@
             jax.ShapeDtypeStruct((species, rows, points), F32),
             jax.ShapeDtypeStruct((species, musc_rows, points), F32),
         ),
-        in_specs=[anywhere] * 6,
+        in_specs=[anywhere] * 8,
         out_specs=(anywhere, anywhere),
         scratch_shapes=[
             pltpu.VMEM((2, species, rows, points), F32),
@@ -514,7 +532,10 @@
             pltpu.VMEM((n, 1, points), jnp.int32),
             pltpu.VMEM((species, points, points), F32),
             pltpu.VMEM((species, points, points), F32),
-            dma((6,)), dma, dma((2,)), dma((2,)),
+            pltpu.VMEM((slots, n), jnp.int32),
+            pltpu.VMEM((slots, n), jnp.int32),
+            pltpu.VMEM((1, n), jnp.int32),
+            dma((8,)), dma, dma((2,)), dma((2,)),
             dma((2,)), dma((2, 2)), dma((2,)), dma((2, 2)),
             dma((2,)),
             pltpu.VMEM((2, 2, species, width - width // 2, points), F32),
@@ -528,7 +549,7 @@
         endothelium.reshape(species, rows, points),
         muscle.reshape(species, musc_rows, points),
         agonist.reshape(rows, points),
-        meta[:, None, :],
+        proj_target[0].T, proj_cell[0].T, proj_count,
         endo_inverse, muscle_inverse,
     )
     endo_next, musc_next = pl.pallas_call(
@@ -539,7 +560,11 @@
         ),
         in_specs=[anywhere] * 2,
         out_specs=(anywhere, anywhere),
-        scratch_shapes=[dma((2, species))],
+        scratch_shapes=[
+            pltpu.VMEM((species, rows, points), F32),
+            pltpu.VMEM((species, musc_rows, points), F32),
+            dma((2, species)), dma((2, species)),
+        ],
         compiler_params=pltpu.CompilerParams(vmem_limit_bytes=60 * 1024 * 1024),
         name="hand_over",
     )(endo_next, musc_next)

time: 130 us -> 81.1 us (0.62)
  Pallas kernels: 127 us -> 80.3 us
  local copies, waits for them, and re-layouts: 1.34 us -> 0 us
    pallas_call x1, Pallas kernels: 48.8 us -> 2.19 us  [local(): pl.pallas_call(hand_over, out_shape=(jax.ShapeDtypeStruct((species, rows,...]
    unnamed x6 -> x0, local copies, waits for them, and re-layouts: 1.34 us -> none
where the time goes in v5:
time: 81.1 us; the launch traced here: 81 us
  Pallas kernels  80.3 us (99%)
    pallas_call x1, Pallas kernels, local(): pl.pallas_call(body, out_shape=(jax.ShapeDtypeStruct((species, rows, poin...  78.1 us
    pallas_call x1, Pallas kernels, local(): pl.pallas_call(hand_over, out_shape=(jax.ShapeDtypeStruct((species, rows,...  2.19 us

profile of v5, /device:TPU:1, one launch (start us, length us, event | category | flops | bytes accessed | tf_op | source)
XLA Modules:
  0.0 81.0 jit_solution(14272119749435172729)
XLA Ops:
  0.6 78.1 %cable_steps.1 = (f32[3,512,128]{2,1,0:T(8,128)}, f32[3,512,128]{2,1,0:T(8,128)}) custom-call(f32[3,512,128]{2,1,0:T(8,128)} %bitcast.11, f32[3,512,128]{2,1,0:T(8,128)} %bitcast.12, f32[512,128]{1,0:T(8,128)} %bitcast.13, s32[2,32]{1,0:T(2,128)} %bitcast.14, s32[2,32]{1,0:T(2,128)} %bitcast.15, s32[1,32]{1,0:T(1,128)} %count_in.1, ...), custom_call_target="tpu_custom_call" | custom-call | tf_op jit(solution)/shard_map/cable_steps/pallas_call | solution.py:500
  78.8 2.2 %hand_over.1 = (f32[3,512,128]{2,1,0:T(8,128)}, f32[3,512,128]{2,1,0:T(8,128)}) custom-call(f32[3,512,128]{2,1,0:T(8,128)} %get-tuple-element.6.endo_from, f32[3,512,128]{2,1,0:T(8,128)} %get-tuple-element.7.musc_from), custom_call_target="tpu_custom_call" | custom-call | tf_op jit(solution)/shard_map/hand_over/pallas_call | solution.py:555

commit v6 on v5

--- a/solution.py
+++ b/solution.py
@@ -432,14 +432,14 @@
         par = lax.rem(t, 2)
         nxt = 1 - par
         local_part(par, nxt, False)
+        pl.when(t > 0)(lambda: messages(nxt).wait_send())
         collect(par)
         endo_outside(par)
+        musc_outside(par)
+        pick()
+        pack(nxt)
         finish_ends(nxt)
         start_far(nxt)
-        musc_outside(par)
-        pick()
-        pl.when(t > 0)(lambda: messages(nxt).wait_send())
-        pack(nxt)
         launch(nxt)
         start_ends(nxt)
         finish_musc(nxt)

time: 81.1 us -> 79 us (0.974)
  Pallas kernels: 80.3 us -> 77.4 us
    pallas_call x1, Pallas kernels: 78.1 us -> 75.3 us  [local(): pl.pallas_call(body, out_shape=(jax.ShapeDtypeStruct((species, rows, poin...]
where the time goes in v6:
time: 79 us; the launch traced here: 78.1 us
  Pallas kernels  77.4 us (98%)
    pallas_call x1, Pallas kernels, local(): pl.pallas_call(body, out_shape=(jax.ShapeDtypeStruct((species, rows, poin...  75.3 us
    pallas_call x1, Pallas kernels, local(): pl.pallas_call(hand_over, out_shape=(jax.ShapeDtypeStruct((species, rows,...  2.19 us

profile of v6, /device:TPU:1, one launch (start us, length us, event | category | flops | bytes accessed | tf_op | source)
XLA Modules:
  0.0 78.1 jit_solution(2309476087508569798)
XLA Ops:
  0.6 75.3 %cable_steps.1 = (f32[3,512,128]{2,1,0:T(8,128)}, f32[3,512,128]{2,1,0:T(8,128)}) custom-call(f32[3,512,128]{2,1,0:T(8,128)} %bitcast.11, f32[3,512,128]{2,1,0:T(8,128)} %bitcast.12, f32[512,128]{1,0:T(8,128)} %bitcast.13, s32[2,32]{1,0:T(2,128)} %bitcast.14, s32[2,32]{1,0:T(2,128)} %bitcast.15, s32[1,32]{1,0:T(1,128)} %count_in.1, ...), custom_call_target="tpu_custom_call" | custom-call | tf_op jit(solution)/shard_map/cable_steps/pallas_call | solution.py:500
  75.9 2.2 %hand_over.1 = (f32[3,512,128]{2,1,0:T(8,128)}, f32[3,512,128]{2,1,0:T(8,128)}) custom-call(f32[3,512,128]{2,1,0:T(8,128)} %get-tuple-element.6.endo_from, f32[3,512,128]{2,1,0:T(8,128)} %get-tuple-element.7.musc_from), custom_call_target="tpu_custom_call" | custom-call | tf_op jit(solution)/shard_map/hand_over/pallas_call | solution.py:555
